TPU v7x, 32 devices: a whole 2x2x4 slice. The times are simulated.
32 devices in a mesh: rows: 16 (over z, y, x), cols: 2 (over core).
Axes of the slice: x: 2, y: 2, z: 4, core: 2. Of those that a mesh axis runs over, the one named last changes fastest.
Arguments:
- descriptors: bfloat16 [16384, 512], P('rows'), may hold values from -17 to 17, as said below
- sparse_points: bfloat16 [2048, 512], P('cols'), may hold values from -0.25 to 0.25
Outputs:
- q_factor: float32 [16384, 256], P('rows')
- r_rows: float32 [256, 2048], P(None, 'cols')
- trailing: bfloat16 [16384, 2048], P('rows', 'cols')
Inputs may be any that keep to these rules, and one draw needn't show every extreme that they name: `descriptors`: each row is a random vector times a positive scale of its own.
All inputs are finite; a program needn't handle non-finite values.
Results may differ from a plain program's by a relative error of at most 0.001.
Values may be sent and summed in bfloat16 or wider, within the bound.
A program may use at most 64 MiB of HBM per device.

v0:
```python
import jax
import jax.numpy as jnp
from jax import lax
from jax.sharding import PartitionSpec as P

PANEL = 128


HIGHEST_PRECISION = lax.Precision.HIGHEST


def spread(value, axis, root):
    mine = lax.axis_index(axis) == root
    return lax.psum(jnp.where(mine, value, jnp.zeros_like(value)), axis)


def transposed_product(first_matrix, second_matrix):
    return lax.dot_general(
        first_matrix,
        second_matrix,
        (((0,), (0,)), ((), ())),
        precision=HIGHEST_PRECISION,
        preferred_element_type=jnp.float32,
    )


def plain_product(first_matrix, second_matrix):
    return jnp.dot(
        first_matrix, second_matrix, precision=HIGHEST_PRECISION, preferred_element_type=jnp.float32
    )


def orthogonal(lower, panel):
    return lax.linalg.triangular_solve(lower, panel.T, left_side=True, lower=True).T


def squared_dots(descriptors, points):
    inner_dots = lax.dot_general(
        descriptors, points, (((1,), (1,)), ((), ())), preferred_element_type=jnp.float32
    )
    return inner_dots * inner_dots


def on_device(descriptors, sparse_points):
    kernel_block = squared_dots(descriptors, sparse_points)
    total_rows = descriptors.shape[0] * lax.axis_size("rows")
    panel_first = spread(kernel_block[:, :PANEL], "cols", 0)
    panel_raw = spread(kernel_block[:, :PANEL], "cols", 1)
    joined = jnp.concatenate([panel_first, panel_raw], axis=1)
    gram_matrix = lax.psum(transposed_product(joined, joined), "rows") / total_rows
    lower_first = jnp.linalg.cholesky(gram_matrix[:PANEL, :PANEL])
    coupling = lax.linalg.triangular_solve(
        lower_first, gram_matrix[:PANEL, PANEL:], left_side=True, lower=True
    )
    schur_block = gram_matrix[PANEL:, PANEL:] - transposed_product(coupling, coupling)
    lower_second = jnp.linalg.cholesky(schur_block)
    q_first = orthogonal(lower_first, panel_first)
    q_second = orthogonal(lower_second, panel_raw - plain_product(q_first, coupling))
    q_joined = jnp.concatenate([q_first, q_second], axis=1)
    r_joined = lax.psum(transposed_product(q_joined, kernel_block), "rows") / total_rows
    remainder = kernel_block - plain_product(q_joined, r_joined)
    return (q_joined, r_joined, remainder.astype(jnp.bfloat16))


def solution(mesh):
    in_specs = (P("rows", None), P("cols", None))
    out_specs = (P("rows", None), P(None, "cols"), P("rows", "cols"))
    return jax.shard_map(
        on_device, mesh=mesh, in_specs=in_specs, out_specs=out_specs, check_vma=False
    )
```

profile of v0, /device:TPU:0, one launch (start us, length us, event | category | flops | bytes accessed | tf_op | source)
XLA Modules:
  0.0 334.3 jit_solution(14562412844431003323)
XLA Ops:
  7.2 0.0 all-reduce.9.cloned.1.call-start
  7.2 1.2 copy-done
  8.4 2.5 convolution_multiply_fusion
  10.9 1.9 copy-done.1
  12.8 1.0 slice_select_fusion.1
  13.9 0.0 all-reduce.5.cloned.1.call-start
  14.0 22.5 %all-reduce.9.cloned.1.call-done = (f32[1024,128]{1,0:T(8,128)}, f32[1024,128]{1,0:T(8,128)}) async-done(((f32[1024,128]{1,0:T(8,128)}, f32[1024,128]{1,0:T(8,128)}), (f32[1024,128]{1,0:T(8,128)}, f32[1024,128]{1,0:T(8,128)})) %all-reduce.9.cloned.1.call-update) | async-done | bytes 1048592 | tf_op jit(solution)/shard_map/psum | solution.py:14
  36.4 4.1 %fusion.1 = f32[256,256]{0,1:T(8,128)} fusion(f32[1024,128]{1,0:T(8,128)} %get-tuple-element.8, f32[1024,128]{1,0:T(8,128)} %get-tuple-element.9), kind=kOutput, calls=%fused_computation.6 | convolution fusion | flops 805568512 | bytes 1310720 | tf_op jit(solution)/shard_map/dot_general | solution.py:18
  40.5 0.2 all-reduce.7.cloned.1.call-start
  40.8 110.2 %all-reduce.5.cloned.1.call-done = f32[256,256]{0,1:T(8,128)} async-done(((f32[256,256]{0,1:T(8,128)}), f32[256,256]{0,1:T(8,128)}) %all-reduce.5.cloned.1.call-update) | async-done | bytes 262160 | tf_op jit(solution)/shard_map/psum | solution.py:50
  151.0 1.0 broadcast_multiply_fusion.1
  151.9 0.1 copy.6
  152.1 11.7 %cholesky.44 = f32[128,128]{1,0:T(8,128)S(1)} custom-call(f32[128,128]{1,0:T(8,128)S(1)} %fusion.15), custom_call_target="Cholesky" | custom-call | tf_op jit(solution)/shard_map/jit(cholesky)/cholesky | solution.py:51
  163.8 0.6 compare_reduce_fusion.1
  164.5 0.7 fusion.7
  165.1 9.8 %custom-call.10 = f32[1,128,128]{1,2,0:T(8,128)S(1)} custom-call(f32[1,128,128]{2,1,0:T(8,128)S(1)} %fusion.7), custom_call_target="InvertDiagBlocksLowerTriangular" | custom-call | tf_op jit(solution)/shard_map/triangular_solve/custom-call.0 | solution.py:34
  174.9 1.7 fusion.5
  176.6 0.3 fusion.9
  176.9 0.3 convolution_subtract_fusion.1
  177.2 1.0 fusion
  178.2 0.1 copy.8
  178.3 11.7 %cholesky.55 = f32[128,128]{1,0:T(8,128)S(1)} custom-call(f32[128,128]{1,0:T(8,128)S(1)} %fusion.12), custom_call_target="Cholesky" | custom-call | tf_op jit(solution)/shard_map/jit(cholesky)/cholesky | solution.py:56
  190.1 0.6 compare_reduce_fusion
  190.7 0.7 fusion.8
  191.4 9.9 %custom-call.11 = f32[1,128,128]{1,2,0:T(8,128)S(1)} custom-call(f32[1,128,128]{2,1,0:T(8,128)S(1)} %fusion.8), custom_call_target="InvertDiagBlocksLowerTriangular" | custom-call | tf_op jit(solution)/shard_map/triangular_solve/custom-call.0 | solution.py:34
  201.3 0.6 convolution_bitcast_fusion
  201.9 6.8 %fusion.17 = f32[256,1024]{1,0:T(8,128)} fusion(f32[1024,1024]{1,0:T(8,128)} %copy-done.1, f32[1024,128]{0,1:T(8,128)S(1)} %convolution_bitcast_fusion, f32[1024,128]{0,1:T(8,128)S(1)} %bitcast.39), kind=kOutput, calls=%fused_computation.37 | convolution fusion | flops 3221487616 | bytes 6291456 | tf_op jit(solution)/shard_map/dot_general | solution.py:18
  208.8 0.1 pad_maximum_fusion
  208.9 1.3 copy.9
  210.2 109.5 %all-reduce.7.cloned.1.call-done = f32[256,1024]{1,0:T(8,128)} async-done(((f32[256,1024]{1,0:T(8,128)}), f32[256,1024]{1,0:T(8,128)}) %all-reduce.7.cloned.1.call-update) | async-done | bytes 1048592 | tf_op jit(solution)/shard_map/psum | solution.py:60
  319.7 1.3 broadcast_multiply_fusion
  321.1 6.7 %subtract_convert_fusion = bf16[1024,1024]{1,0:T(8,128)(2,1)} fusion(f32[1024,1024]{1,0:T(8,128)} %copy-done.1, f32[256,1024]{1,0:T(8,128)S(1)} %broadcast_multiply_fusion, f32[1024,128]{0,1:T(8,128)S(1)} %convolution_bitcast_fusion, f32[1024,128]{0,1:T(8,128)S(1)} %bitcast.41), kind=kOutput, calls=%fused_computation | convolution fusion | flops 3223584768 | bytes 8388608 | tf_op jit(solution)/shard_map/dot_general | solution.py:28
  (14 shorter events, 0.2 us)
Async XLA Ops:
  7.2 1.2 copy-start
  7.2 29.2 %all-reduce.9.cloned.1.call-start = ((), (), s32[]{:S(2)}) async-start(), calls=%async_computation.2 | async-start | bytes 2097152 | tf_op jit(solution)/shard_map/psum | solution.py:14
  10.9 1.9 copy-start.1
  13.9 137.1 %all-reduce.5.cloned.1.call-start = ((), (), s32[]{:S(2)}) async-start(), calls=%async_computation | async-start | bytes 524288 | tf_op jit(solution)/shard_map/psum | solution.py:50
  36.4 140.8 %copy-start.3 = (f32[1024,128]{1,0:T(8,128)S(1)}, f32[1024,128]{1,0:T(8,128)}, u32[]{:S(2)}) copy-start(f32[1024,128]{1,0:T(8,128)} %get-tuple-element.8) | copy-start | bytes 1572868
  40.5 279.2 %all-reduce.7.cloned.1.call-start = ((), (), s32[]{:S(2)}) async-start(), calls=%async_computation.1 | async-start | bytes 2097152 | tf_op jit(solution)/shard_map/psum | solution.py:60
  321.0 6.7 %copy-start.2 = (f32[256,1024]{1,0:T(8,128)}, f32[256,1024]{1,0:T(8,128)S(1)}, u32[]{:S(2)}) copy-start(f32[256,1024]{1,0:T(8,128)S(1)} %broadcast_multiply_fusion) | copy-start | bytes 3145732
Sparse Core Ops, SparseCore 0:
  14.0 22.3 all-reduce.8
  43.0 107.8 all-reduce.4
  208.9 110.7 all-reduce.6
where the time goes:
time: 335 us; the launch traced here: 334 us
  waiting for transfers between devices  242 us (72%)
  other arithmetic  49.3 us (15%)
  matrix products  24 us (7%)
  between operations  13.9 us (4%)
  local copies, waits for them, and re-layouts  4.59 us (1%)
    psum x1, waiting for transfers between devices, on_device(): lax.psum(transposed_product(joined, joined), 'rows') / total_rows  110 us
    psum x1, waiting for transfers between devices, on_device(): lax.psum(transposed_product(q_joined, kernel_block), 'rows') / total_rows  109 us
    psum x1, waiting for transfers between devices, spread(): return lax.psum(jnp.where(mine, value, jnp.zeros_like(value)), axis)  22.5 us
    another operation x4, other arithmetic, orthogonal(): lax.linalg.triangular_solve(lower, panel.T, left_side=True, lower=True)  21 us
    another operation x3, other arithmetic, on_device(): lower_first = jnp.linalg.cholesky(gram_matrix[:PANEL, :PANEL])  12.4 us
    another operation x3, other arithmetic, on_device(): lower_second = jnp.linalg.cholesky(schur_block)  12.4 us
    dot_general x3, matrix products, transposed_product(): lax.dot_general(first_matrix, second_matrix, (((0,), (0,)), ((), ())), pr...  11.2 us
    dot_general x2, matrix products, plain_product(): jnp.dot(first_matrix, second_matrix, precision=HIGHEST_PRECISION, preferr...  7.7 us
  transfers between devices with their start and end apart: 3, of which 3 were waited for; matrix products, arithmetic and copies ran while one was open for 0% of the time, Pallas kernels for 0%

commit v1 on v0

v1 whole, which is shorter than its diff:
```python
import functools

import jax
import jax.numpy as jnp
from jax import lax
from jax.experimental import pallas as pl
from jax.experimental.pallas import tpu as pltpu
from jax.sharding import PartitionSpec as P

PANEL = 128
BLOCK = 32
LANES = 128
HIGHEST = lax.Precision.HIGHEST
F32 = jnp.float32
BF16 = jnp.bfloat16
MESH = pl.DeviceIdType.MESH


def dot_nt(a, b, precision=None):
    return lax.dot_general(
        a, b, (((1,), (1,)), ((), ())), precision=precision, preferred_element_type=F32
    )


def dot_nn(a, b, precision=None):
    return lax.dot_general(
        a, b, (((1,), (0,)), ((), ())), precision=precision, preferred_element_type=F32
    )


def dot_tn(a, b, precision=None):
    return lax.dot_general(
        a, b, (((0,), (0,)), ((), ())), precision=precision, preferred_element_type=F32
    )


def split(value):
    high = value.astype(BF16)
    return high, (value - high.astype(F32)).astype(BF16)


def three_pass(a_high, a_low, b_high, b_low):
    return dot_nn(a_high, b_high) + (dot_nn(a_high, b_low) + dot_nn(a_low, b_high))


def factor_block(work, at):
    tile_at, off = at // LANES * LANES, at % LANES
    tile = work[at : at + BLOCK, tile_at : tile_at + LANES]
    row = lax.broadcasted_iota(jnp.int32, (BLOCK, LANES), 0)
    lane = lax.broadcasted_iota(jnp.int32, (BLOCK, LANES), 1)
    rows = lax.broadcasted_iota(jnp.int32, (BLOCK, 1), 0)
    inverse = jnp.where(row == lane, 1.0, 0.0).astype(F32)
    for j in range(BLOCK - 1):
        column = tile[:, off + j : off + j + 1]
        pivot = tile[j : j + 1, off + j : off + j + 1]
        factor = jnp.where(rows > j, column / pivot, 0.0)
        tile = tile - factor * tile[j : j + 1, :]
        inverse = inverse - factor * inverse[j : j + 1, :]
    pivots = jnp.sum(jnp.where(lane == row + off, tile, 0.0), axis=1, keepdims=True)
    return (inverse * lax.rsqrt(pivots))[:, :BLOCK]


def factor_step(work, at):
    size = work.shape[0]
    panel = dot_nn(factor_block(work, at), work[at : at + BLOCK, :], HIGHEST)
    work[at : at + BLOCK, :] = panel
    rest = at + BLOCK
    if rest < size:
        start = rest // LANES * LANES
        change = dot_tn(panel[:, start:size], panel, HIGHEST)
        work[rest:size, :] = work[rest:size, :] - change[rest - start :, :]


def reduce_kernel(
    n_rows, n_cols, inner, total_rows,
    d_ref, p_ref, pp_ref, s_ref, linv_ref,
    pp, k_high, k_low, part, full, recv_one, recv_two, gram_one, gram_two, gram_own, gram, work,
    pp_send, pp_recv, sends, recvs, grams_send, grams_recv, swap_send, swap_recv, out_sem,
):
    outer = n_rows // inner
    me_row, me_col = lax.axis_index("rows"), lax.axis_index("cols")
    me_in, me_out = lax.rem(me_row, inner), lax.div(me_row, inner)
    joint = 2 * PANEL
    blocks = part.shape[0] // joint

    def inner_peer(t):
        at = lax.rem(me_in + t, inner)
        return at, (me_out * inner + at, me_col)

    def outer_peer(t):
        at = lax.rem(me_out + t, outer)
        return at, (at * inner + me_in, me_col)

    barrier = pltpu.get_barrier_semaphore()
    for t in range(1, inner):
        pl.semaphore_signal(barrier, inc=1, device_id=inner_peer(t)[1], device_id_type=MESH)
    for t in range(1, outer):
        pl.semaphore_signal(barrier, inc=1, device_id=outer_peer(t)[1], device_id_type=MESH)
    for t in range(1, n_cols):
        to = lax.rem(me_col + t, n_cols)
        pl.semaphore_signal(barrier, inc=1, device_id=(me_row, to), device_id_type=MESH)
    pl.semaphore_wait(barrier, inner + outer + n_cols - 3)

    def share(source, target_of, send_sem, recv_sem, own):
        def copy(which, t):
            to = lax.rem(which + t, n_cols)
            return pltpu.make_async_remote_copy(
                src_ref=source, dst_ref=target_of(which),
                send_sem=send_sem.at[which, t - 1], recv_sem=recv_sem.at[which],
                device_id=(me_row, to), device_id_type=MESH,
            )

        def start():
            for which in range(2):
                @pl.when(me_col == which)
                def _():
                    for t in range(1, n_cols):
                        copy(which, t).start()
                    own(which)

        def finish():
            for which in range(2):
                @pl.when(me_col != which)
                def _():
                    copy(which, 1).wait_recv()

        def drain():
            for which in range(2):
                @pl.when(me_col == which)
                def _():
                    for t in range(1, n_cols):
                        copy(which, t).wait_send()

        return start, finish, drain

    def own_points(which):
        pp[which * PANEL : (which + 1) * PANEL, :] = p_ref[:PANEL, :]

    points_start, points_finish, points_drain = share(
        p_ref.at[pl.ds(0, PANEL)],
        lambda which: pp.at[pl.ds(which * PANEL, PANEL)],
        pp_send, pp_recv, own_points,
    )
    points_start()
    for block in range(blocks // 2):
        cols = slice(block * joint, (block + 1) * joint)
        dots = dot_nt(d_ref[...], p_ref[cols, :])
        k_high[:, cols], k_low[:, cols] = split(dots * dots)
    points_finish()
    dots = dot_nt(pp[...], d_ref[...])
    j_high, j_low = split(dots * dots)
    pp_ref[...] = pp[...]

    def products(block):
        cols = slice(block * joint, (block + 1) * joint)
        value = three_pass(j_high, j_low, k_high[:, cols], k_low[:, cols])
        part[block * 2 * joint : block * 2 * joint + joint, :] = value[:, :PANEL]
        part[block * 2 * joint + joint : (block + 1) * 2 * joint, :] = value[:, PANEL:]

    piece = joint // inner

    def gram_scatter(t):
        to, device = inner_peer(t)
        return pltpu.make_async_remote_copy(
            src_ref=part.at[pl.ds(pl.multiple_of(to * piece, 8), piece)],
            dst_ref=gram_one.at[t - 1],
            send_sem=grams_send.at[0, t - 1], recv_sem=grams_recv.at[0, t - 1],
            device_id=device, device_id_type=MESH,
        )

    def gram_exchange(t):
        device = outer_peer(t)[1]
        return pltpu.make_async_remote_copy(
            src_ref=gram_two.at[me_out], dst_ref=gram_two.at[me_out],
            send_sem=grams_send.at[1, t - 1], recv_sem=grams_recv.at[1, t - 1],
            device_id=device, device_id_type=MESH,
        )

    own_piece = pl.ds(pl.multiple_of(me_in * piece, 8), piece)

    def gram_gather(t):
        device = inner_peer(t)[1]
        return pltpu.make_async_remote_copy(
            src_ref=gram_own.at[own_piece], dst_ref=gram_own.at[own_piece],
            send_sem=grams_send.at[2, t - 1], recv_sem=grams_recv.at[2, t - 1],
            device_id=device, device_id_type=MESH,
        )

    products(0)
    for t in range(1, inner):
        gram_scatter(t).start()
    for block in range(1, blocks // 2):
        products(block)

    first = joint if (part.shape[0] - joint) % (16 * n_rows) == 0 else 0
    chunk = (part.shape[0] - first) // 2
    wide, narrow = chunk // inner, chunk // n_rows

    def bulk(c):
        base = first + c * chunk

        def wide_at(i):
            return pl.ds(pl.multiple_of(base + i * wide, 8), wide)

        def narrow_at(o):
            return pl.ds(pl.multiple_of(base + me_in * wide + o * narrow, 8), narrow)

        def copy(stage, t):
            to, device = (inner_peer if stage in (0, 3) else outer_peer)(t)
            source, target = (
                (lambda: (part.at[wide_at(to)], recv_one.at[c, t - 1])),
                (lambda: (part.at[narrow_at(to)], recv_two.at[c, t - 1])),
                (lambda: (full.at[narrow_at(me_out)],) * 2),
                (lambda: (full.at[wide_at(me_in)],) * 2),
            )[stage]()
            return pltpu.make_async_remote_copy(
                src_ref=source, dst_ref=target,
                send_sem=sends.at[c, stage, t - 1], recv_sem=recvs.at[c, stage, t - 1],
                device_id=device, device_id_type=MESH,
            )

        def copies(stage):
            return [copy(stage, t) for t in range(1, inner if stage in (0, 3) else outer)]

        def start(stage):
            for one in copies(stage):
                one.start()

        def step(stage):
            for one in copies(stage):
                one.wait_recv()
            if stage == 0:
                for one in copies(stage):
                    one.wait_send()
                value = part[wide_at(me_in), :]
                for t in range(inner - 1):
                    value = value + recv_one[c, t]
                part[wide_at(me_in), :] = value
            if stage == 1:
                value = part[narrow_at(me_out), :]
                for t in range(outer - 1):
                    value = value + recv_two[c, t]
                full[narrow_at(me_out), :] = value
            if stage < 3:
                start(stage + 1)

        def drain():
            for stage in range(1, 4):
                for one in copies(stage):
                    one.wait_send()

        return start, step, drain

    (start_a, step_a, drain_a), (start_b, step_b, drain_b) = bulk(0), bulk(1)

    for t in range(1, inner):
        gram_scatter(t).wait_recv()
    value = part[own_piece, :]
    for t in range(inner - 1):
        value = value + gram_one[t]
    gram_two[me_out] = value
    for t in range(1, outer):
        gram_exchange(t).start()
    for t in range(1, inner):
        gram_scatter(t).wait_send()
    start_a(0)
    for t in range(1, outer):
        gram_exchange(t).wait_recv()
    value = gram_two[0]
    for o in range(1, outer):
        value = value + gram_two[o]
    gram_own[own_piece, :] = value
    for t in range(1, inner):
        gram_gather(t).start()
    start_b(0)
    for t in range(1, inner):
        gram_gather(t).wait_recv()

    def own_gram(which):
        gram[which] = gram_own[...]

    gram_start, gram_finish, gram_drain = share(
        gram_own, lambda which: gram.at[which], swap_send, swap_recv, own_gram
    )
    gram_start()
    gram_finish()
    work[:, :PANEL] = gram[0] / total_rows
    work[:, PANEL:joint] = gram[1] / total_rows
    row = lax.broadcasted_iota(jnp.int32, (joint, joint), 0)
    lane = lax.broadcasted_iota(jnp.int32, (joint, joint), 1)
    work[:, joint:] = jnp.where(row == lane, 1.0, 0.0).astype(F32)

    pending = [
        functools.partial(step, stage) for stage in range(4) for step in (step_a, step_b)
    ]
    for at in range(0, joint, BLOCK):
        factor_step(work, at)
        if pending and at >= BLOCK:
            pending.pop(0)()
    linv_ref[...] = work[:, joint:]
    for step in pending:
        step()
    rest = pl.ds(first, part.shape[0] - first)
    results = [pltpu.make_async_copy(full.at[rest], s_ref.at[rest], out_sem.at[0])]
    if first > 0:
        head = s_ref.at[pl.ds(0, joint)]
        results.append(pltpu.make_async_copy(gram_own, head, out_sem.at[1]))
    for result in results:
        result.start()
    points_drain()
    gram_drain()
    for t in range(1, outer):
        gram_exchange(t).wait_send()
    for t in range(1, inner):
        gram_gather(t).wait_send()
    drain_a()
    drain_b()
    for result in results:
        result.wait()


def reduced(descriptors, points, n_rows, n_cols):
    rows, width = descriptors.shape
    cols = points.shape[0]
    joint = 2 * PANEL
    inner = 4 if n_rows % 4 == 0 else 1
    outer = n_rows // inner
    flat = cols // PANEL * joint
    first = joint if (flat - joint) % (16 * n_rows) == 0 else 0
    chunk = (flat - first) // 2
    most = max(inner, outer, 2) - 1
    vmem = pl.BlockSpec(memory_space=pltpu.VMEM)
    dma = pltpu.SemaphoreType.DMA
    return pl.pallas_call(
        functools.partial(reduce_kernel, n_rows, n_cols, inner, float(rows * n_rows)),
        out_shape=(
            jax.ShapeDtypeStruct((joint, width), BF16),
            jax.ShapeDtypeStruct((flat, PANEL), F32),
            jax.ShapeDtypeStruct((joint, joint), F32),
        ),
        in_specs=[vmem, vmem],
        out_specs=(vmem, pl.BlockSpec(memory_space=pl.ANY), vmem),
        scratch_shapes=[
            pltpu.VMEM((joint, width), BF16),
            pltpu.VMEM((rows, cols), BF16),
            pltpu.VMEM((rows, cols), BF16),
            pltpu.VMEM((flat, PANEL), F32),
            pltpu.VMEM((flat, PANEL), F32),
            pltpu.VMEM((2, inner - 1, chunk // inner, PANEL), F32),
            pltpu.VMEM((2, outer - 1, chunk // n_rows, PANEL), F32),
            pltpu.VMEM((inner - 1, joint // inner, PANEL), F32),
            pltpu.VMEM((outer, joint // inner, PANEL), F32),
            pltpu.VMEM((joint, PANEL), F32),
            pltpu.VMEM((2, joint, PANEL), F32),
            pltpu.VMEM((joint, 2 * joint), F32),
            dma((2, n_cols - 1)),
            dma((2,)),
            dma((2, 4, most)),
            dma((2, 4, most)),
            dma((3, most)),
            dma((3, most)),
            dma((2, n_cols - 1)),
            dma((2,)),
            dma((2,)),
        ],
        compiler_params=pltpu.CompilerParams(
            collective_id=0, has_side_effects=True, vmem_limit_bytes=40 * 1024 * 1024
        ),
        name="gram_and_products",
    )(descriptors, points)


def finish_kernel(
    total_rows, d_ref, p_ref, pp_ref, s_ref, linv_ref, q_ref, r_ref, t_ref, r_high, r_low
):
    joint = 2 * PANEL

    @pl.when(pl.program_id(0) == 0)
    def _():
        for block in range(r_ref.shape[1] // PANEL):
            cols = slice(block * PANEL, (block + 1) * PANEL)
            sums = s_ref[block * joint : (block + 1) * joint, :]
            value = dot_nn(linv_ref[...], sums, HIGHEST) / total_rows
            r_ref[:, cols] = value
            r_high[:, cols], r_low[:, cols] = split(value)

    dots = dot_nt(d_ref[...], pp_ref[...])
    q = dot_nt(dots * dots, linv_ref[...], HIGHEST)
    q_ref[...] = q
    q_high, q_low = split(q)
    for block in range(r_ref.shape[1] // joint):
        cols = slice(block * joint, (block + 1) * joint)
        dots = dot_nt(d_ref[...], p_ref[cols, :])
        change = three_pass(q_high, q_low, r_high[:, cols], r_low[:, cols])
        t_ref[:, cols] = (dots * dots - change).astype(BF16)


def finished(descriptors, points, panel_points, sums, inverse, total_rows):
    rows, width = descriptors.shape
    cols = points.shape[0]
    joint = 2 * PANEL
    tile = 256
    whole = lambda shape: pl.BlockSpec(shape, lambda i: (0, 0))
    tiled = lambda lanes: pl.BlockSpec((tile, lanes), lambda i: (i, 0))
    return pl.pallas_call(
        functools.partial(finish_kernel, total_rows),
        out_shape=(
            jax.ShapeDtypeStruct((rows, joint), F32),
            jax.ShapeDtypeStruct((joint, cols), F32),
            jax.ShapeDtypeStruct((rows, cols), BF16),
        ),
        grid=(rows // tile,),
        in_specs=[
            tiled(width),
            whole((cols, width)),
            whole((joint, width)),
            whole(sums.shape),
            whole((joint, joint)),
        ],
        out_specs=(tiled(joint), whole((joint, cols)), tiled(cols)),
        scratch_shapes=[pltpu.VMEM((joint, cols), BF16), pltpu.VMEM((joint, cols), BF16)],
        compiler_params=pltpu.CompilerParams(vmem_limit_bytes=40 * 1024 * 1024),
        name="factors_and_remainder",
    )(descriptors, points, panel_points, sums, inverse)


def solution(mesh):
    n_rows, n_cols = mesh.shape["rows"], mesh.shape["cols"]

    def on_device(descriptors, sparse_points):
        panel_points, sums, inverse = reduced(descriptors, sparse_points, n_rows, n_cols)
        total_rows = float(descriptors.shape[0] * n_rows)
        return finished(descriptors, sparse_points, panel_points, sums, inverse, total_rows)

    in_specs = (P("rows", None), P("cols", None))
    out_specs = (P("rows", None), P(None, "cols"), P("rows", "cols"))
    return jax.shard_map(
        on_device, mesh=mesh, in_specs=in_specs, out_specs=out_specs, check_vma=False
    )
```

time: 335 us -> 70.4 us (0.21)
  waiting for transfers between devices: 242 us -> 0 us
  Pallas kernels: 0 us -> 67.1 us
  other arithmetic: 49.3 us -> 0 us
  matrix products: 24 us -> 0 us
  between operations: 13.9 us -> 0.65 us
    psum x3 -> x0, waiting for transfers between devices: 242 us -> none  [the longest x1 110 us: on_device(): lax.psum(transposed_product(joined, joined), 'rows') / total_rows]
    pallas_call x0 -> x2, Pallas kernels: none -> 67.1 us  [the longest x1 58.7 us: reduced(): pl.pallas_call(functools.partial(reduce_kernel, n_rows, n_cols, inner, fl...]
    another operation x10 -> x0, other arithmetic: 45.8 us -> none  [the longest x4 21 us: orthogonal(): lax.linalg.triangular_solve(lower, panel.T, left_side=True, lower=True)]
    dot_general x6 -> x0, matrix products: 21.4 us -> none  [the longest x3 11.2 us: transposed_product(): lax.dot_general(first_matrix, second_matrix, (((0,), (0,)), ((), ())), pr...]
  transfers between devices with their start and end apart: 3 -> 0, of which waited for: 3 -> 0; matrix products, arithmetic and copies ran while one was open for 0% -> 0% of each run, Pallas kernels for 0% -> 0%
where the time goes in v1:
time: 70.4 us; the launch traced here: 70.2 us
  Pallas kernels  67.1 us (95%)
  local copies, waits for them, and re-layouts  2.44 us (3%)
    pallas_call x1, Pallas kernels, reduced(): pl.pallas_call(functools.partial(reduce_kernel, n_rows, n_cols, inner, fl...  58.7 us
    pallas_call x1, Pallas kernels, finished(): pl.pallas_call(functools.partial(finish_kernel, total_rows), out_shape=(j...  8.33 us
    unnamed x4, local copies, waits for them, and re-layouts  2.44 us

profile of v1, /device:TPU:0, one launch (start us, length us, event | category | flops | bytes accessed | tf_op | source)
XLA Modules:
  0.0 70.2 jit_solution(3990767236401352862)
XLA Ops:
  0.6 0.0 copy-start
  0.6 1.2 %copy-done = bf16[1024,512]{1,0:T(8,128)(2,1)S(1)} copy-done((bf16[1024,512]{1,0:T(8,128)(2,1)S(1)}, bf16[1024,512]{1,0:T(8,128)(2,1)}, u32[]{:S(2)}) %copy-start) | copy-done | bytes 1048600
  1.9 0.0 copy-start.1
  1.9 1.2 %copy-done.1 = bf16[1024,512]{1,0:T(8,128)(2,1)S(1)} copy-done((bf16[1024,512]{1,0:T(8,128)(2,1)S(1)}, bf16[1024,512]{1,0:T(8,128)(2,1)}, u32[]{:S(2)}) %copy-start.1) | copy-done | bytes 1048600
  3.1 58.7 %gram_and_products.1 = (bf16[256,512]{1,0:T(8,128)(2,1)S(1)}, f32[2048,128]{1,0:T(8,128)S(1)}, f32[256,256]{1,0:T(8,128)S(1)}) custom-call(bf16[1024,512]{1,0:T(8,128)(2,1)S(1)} %copy-done, bf16[1024,512]{1,0:T(8,128)(2,1)S(1)} %copy-done.1), custom_call_target="tpu_custom_call" | custom-call | tf_op jit(solution)/shard_map/gram_and_products/pallas_call | solution.py:334
  61.8 8.3 %factors_and_remainder.1 = (f32[1024,256]{1,0:T(8,128)}, f32[256,1024]{1,0:T(8,128)}, bf16[1024,1024]{1,0:T(8,128)(2,1)}) custom-call(bf16[1024,512]{1,0:T(8,128)(2,1)S(1)} %copy-done, bf16[1024,512]{1,0:T(8,128)(2,1)S(1)} %copy-done.1, bf16[256,512]{1,0:T(8,128)(2,1)S(1)} %get-tuple-element.6.pp_ref, f32[2048,128]{1,0:T(8,128)S(1)} %get-tuple-element.7.s_ref, ...), custom_call_target="tpu_custom_call" | custom-call | tf_op jit(solution)/shard_map/factors_and_remainder/pallas_call | solution.py:405
Async XLA Ops:
  0.6 1.2 %copy-start = (bf16[1024,512]{1,0:T(8,128)(2,1)S(1)}, bf16[1024,512]{1,0:T(8,128)(2,1)}, u32[]{:S(2)}) copy-start(bf16[1024,512]{1,0:T(8,128)(2,1)} %d_ref.3) | copy-start | bytes 3145732
  1.9 1.2 %copy-start.1 = (bf16[1024,512]{1,0:T(8,128)(2,1)S(1)}, bf16[1024,512]{1,0:T(8,128)(2,1)}, u32[]{:S(2)}) copy-start(bf16[1024,512]{1,0:T(8,128)(2,1)} %p_ref.3) | copy-start | bytes 3145732

commit v2 on v1

--- a/solution.py
+++ b/solution.py
@@ -9,6 +9,7 @@
 
 PANEL = 128
 BLOCK = 32
+SUB = 8
 LANES = 128
 HIGHEST = lax.Precision.HIGHEST
 F32 = jnp.float32
@@ -43,39 +44,54 @@
     return dot_nn(a_high, b_high) + (dot_nn(a_high, b_low) + dot_nn(a_low, b_high))
 
 
-def factor_block(work, at):
-    tile_at, off = at // LANES * LANES, at % LANES
-    tile = work[at : at + BLOCK, tile_at : tile_at + LANES]
+def factor_block(tile, off):
     row = lax.broadcasted_iota(jnp.int32, (BLOCK, LANES), 0)
     lane = lax.broadcasted_iota(jnp.int32, (BLOCK, LANES), 1)
-    rows = lax.broadcasted_iota(jnp.int32, (BLOCK, 1), 0)
     inverse = jnp.where(row == lane, 1.0, 0.0).astype(F32)
-    for j in range(BLOCK - 1):
-        column = tile[:, off + j : off + j + 1]
-        pivot = tile[j : j + 1, off + j : off + j + 1]
-        factor = jnp.where(rows > j, column / pivot, 0.0)
-        tile = tile - factor * tile[j : j + 1, :]
-        inverse = inverse - factor * inverse[j : j + 1, :]
-    pivots = jnp.sum(jnp.where(lane == row + off, tile, 0.0), axis=1, keepdims=True)
-    return (inverse * lax.rsqrt(pivots))[:, :BLOCK]
+    done = []
+    for top in range(0, BLOCK, SUB):
+        left = BLOCK - top
+        rows = row[:left, :]
+        columns = [
+            jnp.broadcast_to(tile[:, off + top + j : off + top + j + 1], (left, LANES))
+            for j in range(SUB)
+        ]
+        scale = jnp.ones((SUB, LANES), F32)
+        for j in range(SUB):
+            pivot = columns[j][j : j + 1, :]
+            factor = jnp.where(rows > j, columns[j] * (1.0 / pivot), 0.0)
+            for k in range(j + 1, SUB):
+                columns[k] = columns[k] - factor * columns[k][j : j + 1, :]
+            tile = tile - factor * tile[j : j + 1, :]
+            inverse = inverse - factor * inverse[j : j + 1, :]
+            scale = jnp.where(rows[:SUB] == j, lax.rsqrt(pivot), scale)
+        done.append(inverse[:SUB] * scale)
+        tile, inverse = tile[SUB:], inverse[SUB:]
+    return jnp.concatenate(done, axis=0)[:, :BLOCK]
 
 
 def factor_step(work, at):
     size = work.shape[0]
-    panel = dot_nn(factor_block(work, at), work[at : at + BLOCK, :], HIGHEST)
-    work[at : at + BLOCK, :] = panel
+    tile_at = at // LANES * LANES
     rest = at + BLOCK
+    start = min(rest // LANES * LANES, size)
+    stop = size + -(-rest // LANES) * LANES
+    factor = factor_block(work[at:rest, tile_at : tile_at + LANES], at - tile_at)
+    panel = dot_nn(factor, work[at:rest, start:stop], HIGHEST)
+    work[at:rest, start:stop] = panel
     if rest < size:
-        start = rest // LANES * LANES
-        change = dot_tn(panel[:, start:size], panel, HIGHEST)
-        work[rest:size, :] = work[rest:size, :] - change[rest - start :, :]
+        turned = panel[:, : size - start].T
+        for low, high in ((rest, rest + BLOCK), (rest + BLOCK, size)):
+            if low < high:
+                change = dot_nn(turned[low - start : high - start, :], panel, HIGHEST)
+                work[low:high, start:stop] = work[low:high, start:stop] - change
 
 
 def reduce_kernel(
     n_rows, n_cols, inner, total_rows,
-    d_ref, p_ref, pp_ref, s_ref, linv_ref,
-    pp, k_high, k_low, part, full, recv_one, recv_two, gram_one, gram_two, gram_own, gram, work,
-    pp_send, pp_recv, sends, recvs, grams_send, grams_recv, swap_send, swap_recv, out_sem,
+    d_hbm, p_hbm, pp_ref, s_ref, linv_ref,
+    d_ref, p_ref, pp, k_high, k_low, part, full, recv_one, recv_two, gram_one, gram_two, gram_own, gram, work,
+    pp_send, pp_recv, sends, recvs, grams_send, grams_recv, swap_send, swap_recv, out_sem, in_sem,
 ):
     outer = n_rows // inner
     me_row, me_col = lax.axis_index("rows"), lax.axis_index("cols")
@@ -99,6 +115,10 @@
     for t in range(1, n_cols):
         to = lax.rem(me_col + t, n_cols)
         pl.semaphore_signal(barrier, inc=1, device_id=(me_row, to), device_id_type=MESH)
+    load_d = pltpu.make_async_copy(d_hbm, d_ref, in_sem.at[0])
+    load_p = pltpu.make_async_copy(p_hbm, p_ref, in_sem.at[1])
+    load_p.start()
+    load_d.start()
     pl.semaphore_wait(barrier, inner + outer + n_cols - 3)
 
     def share(source, target_of, send_sem, recv_sem, own):
@@ -116,10 +136,13 @@
                 def _():
                     for t in range(1, n_cols):
                         copy(which, t).start()
-                    own(which)
 
         def finish():
             for which in range(2):
+                @pl.when(me_col == which)
+                def _():
+                    own(which)
+
                 @pl.when(me_col != which)
                 def _():
                     copy(which, 1).wait_recv()
@@ -137,11 +160,13 @@
         pp[which * PANEL : (which + 1) * PANEL, :] = p_ref[:PANEL, :]
 
     points_start, points_finish, points_drain = share(
-        p_ref.at[pl.ds(0, PANEL)],
+        p_hbm.at[pl.ds(0, PANEL)],
         lambda which: pp.at[pl.ds(which * PANEL, PANEL)],
         pp_send, pp_recv, own_points,
     )
     points_start()
+    load_p.wait()
+    load_d.wait()
     for block in range(blocks // 2):
         cols = slice(block * joint, (block + 1) * joint)
         dots = dot_nt(d_ref[...], p_ref[cols, :])
@@ -338,9 +363,11 @@
             jax.ShapeDtypeStruct((flat, PANEL), F32),
             jax.ShapeDtypeStruct((joint, joint), F32),
         ),
-        in_specs=[vmem, vmem],
+        in_specs=[pl.BlockSpec(memory_space=pltpu.HBM)] * 2,
         out_specs=(vmem, pl.BlockSpec(memory_space=pl.ANY), vmem),
         scratch_shapes=[
+            pltpu.VMEM((rows, width), BF16),
+            pltpu.VMEM((cols, width), BF16),
             pltpu.VMEM((joint, width), BF16),
             pltpu.VMEM((rows, cols), BF16),
             pltpu.VMEM((rows, cols), BF16),
@@ -362,9 +389,10 @@
             dma((2, n_cols - 1)),
             dma((2,)),
             dma((2,)),
+            dma((2,)),
         ],
         compiler_params=pltpu.CompilerParams(
-            collective_id=0, has_side_effects=True, vmem_limit_bytes=40 * 1024 * 1024
+            collective_id=0, has_side_effects=True, vmem_limit_bytes=60 * 1024 * 1024
         ),
         name="gram_and_products",
     )(descriptors, points)

time: 70.4 us -> 63.3 us (0.90)
  Pallas kernels: 67.1 us -> 59.2 us
    pallas_call x1, Pallas kernels: 58.7 us -> 50.9 us  [reduced(): pl.pallas_call(functools.partial(reduce_kernel, n_rows, n_cols, inner, fl...]
    unnamed x4 -> x10, local copies, waits for them, and re-layouts: 2.44 us -> 3.13 us
where the time goes in v2:
time: 63.3 us; the launch traced here: 63 us
  Pallas kernels  59.2 us (94%)
  local copies, waits for them, and re-layouts  3.13 us (5%)
  between operations  0.68 us (1%)
    pallas_call x1, Pallas kernels, reduced(): pl.pallas_call(functools.partial(reduce_kernel, n_rows, n_cols, inner, fl...  50.9 us
    pallas_call x1, Pallas kernels, finished(): pl.pallas_call(functools.partial(finish_kernel, total_rows), out_shape=(j...  8.3 us
    unnamed x10, local copies, waits for them, and re-layouts  3.13 us

profile of v2, /device:TPU:0, one launch (start us, length us, event | category | flops | bytes accessed | tf_op | source)
XLA Modules:
  0.0 63.0 jit_solution(5899139261613287388)
XLA Ops:
  0.6 0.0 copy-start.1
  0.6 0.0 copy-start
  0.6 50.9 %gram_and_products.1 = (bf16[256,512]{1,0:T(8,128)(2,1)}, f32[2048,128]{1,0:T(8,128)}, f32[256,256]{1,0:T(8,128)}) custom-call(bf16[1024,512]{1,0:T(8,128)(2,1)} %d_ref.1, bf16[1024,512]{1,0:T(8,128)(2,1)} %p_ref.1), custom_call_target="tpu_custom_call" | custom-call | tf_op jit(solution)/shard_map/gram_and_products/pallas_call | solution.py:359
  51.6 0.0 copy-done.1
  51.6 0.0 copy-done
  51.6 0.0 copy-start.2
  51.6 1.2 %copy-done.2 = f32[2048,128]{1,0:T(8,128)S(1)} copy-done((f32[2048,128]{1,0:T(8,128)S(1)}, f32[2048,128]{1,0:T(8,128)}, u32[]{:S(2)}) %copy-start.2) | copy-done | bytes 1048600
  52.8 0.0 copy-start.3
  52.8 0.9 %copy-done.3 = bf16[256,512]{1,0:T(8,128)(2,1)S(1)} copy-done((bf16[256,512]{1,0:T(8,128)(2,1)S(1)}, bf16[256,512]{1,0:T(8,128)(2,1)}, u32[]{:S(2)}) %copy-start.3) | copy-done | bytes 262168
  53.8 0.0 copy-start.4
  53.8 0.9 %copy-done.4 = f32[256,256]{1,0:T(8,128)S(1)} copy-done((f32[256,256]{1,0:T(8,128)S(1)}, f32[256,256]{1,0:T(8,128)}, u32[]{:S(2)}) %copy-start.4) | copy-done | bytes 262168
  54.7 8.3 %factors_and_remainder.1 = (f32[1024,256]{1,0:T(8,128)}, f32[256,1024]{1,0:T(8,128)}, bf16[1024,1024]{1,0:T(8,128)(2,1)}) custom-call(bf16[1024,512]{1,0:T(8,128)(2,1)S(1)} %copy-done, bf16[1024,512]{1,0:T(8,128)(2,1)S(1)} %copy-done.1, bf16[256,512]{1,0:T(8,128)(2,1)S(1)} %copy-done.3, f32[2048,128]{1,0:T(8,128)S(1)} %copy-done.2, f32[256,256]{1,0:T(8,128)S(1)} %copy-done.4), custom_call_target="tpu_custom_call" | custom-call | tf_op jit(solution)/shard_map/factors_and_remainder/pallas_call | solution.py:433
Async XLA Ops:
  0.6 51.0 %copy-start.1 = (bf16[1024,512]{1,0:T(8,128)(2,1)S(1)}, bf16[1024,512]{1,0:T(8,128)(2,1)}, u32[]{:S(2)}) copy-start(bf16[1024,512]{1,0:T(8,128)(2,1)} %p_ref.1) | copy-start | bytes 3145732
  0.6 51.0 %copy-start = (bf16[1024,512]{1,0:T(8,128)(2,1)S(1)}, bf16[1024,512]{1,0:T(8,128)(2,1)}, u32[]{:S(2)}) copy-start(bf16[1024,512]{1,0:T(8,128)(2,1)} %d_ref.1) | copy-start | bytes 3145732
  51.6 1.2 %copy-start.2 = (f32[2048,128]{1,0:T(8,128)S(1)}, f32[2048,128]{1,0:T(8,128)}, u32[]{:S(2)}) copy-start(f32[2048,128]{1,0:T(8,128)} %get-tuple-element.7.s_ref) | copy-start | bytes 3145732
  52.8 0.9 %copy-start.3 = (bf16[256,512]{1,0:T(8,128)(2,1)S(1)}, bf16[256,512]{1,0:T(8,128)(2,1)}, u32[]{:S(2)}) copy-start(bf16[256,512]{1,0:T(8,128)(2,1)} %get-tuple-element.6.pp_ref) | copy-start | bytes 786436
  53.8 0.9 %copy-start.4 = (f32[256,256]{1,0:T(8,128)S(1)}, f32[256,256]{1,0:T(8,128)}, u32[]{:S(2)}) copy-start(f32[256,256]{1,0:T(8,128)} %get-tuple-element.8.linv_ref) | copy-start | bytes 786436

commit v3 on v2

--- a/solution.py
+++ b/solution.py
@@ -277,6 +277,8 @@
         return start, step, drain
 
     (start_a, step_a, drain_a), (start_b, step_b, drain_b) = bulk(0), bulk(1)
+    start_a(0)
+    start_b(0)
 
     for t in range(1, inner):
         gram_scatter(t).wait_recv()
@@ -288,7 +290,6 @@
         gram_exchange(t).start()
     for t in range(1, inner):
         gram_scatter(t).wait_send()
-    start_a(0)
     for t in range(1, outer):
         gram_exchange(t).wait_recv()
     value = gram_two[0]
@@ -297,7 +298,7 @@
     gram_own[own_piece, :] = value
     for t in range(1, inner):
         gram_gather(t).start()
-    start_b(0)
+    step_a(0)
     for t in range(1, inner):
         gram_gather(t).wait_recv()
 
@@ -308,6 +309,7 @@
         gram_own, lambda which: gram.at[which], swap_send, swap_recv, own_gram
     )
     gram_start()
+    step_b(0)
     gram_finish()
     work[:, :PANEL] = gram[0] / total_rows
     work[:, PANEL:joint] = gram[1] / total_rows
@@ -316,11 +318,11 @@
     work[:, joint:] = jnp.where(row == lane, 1.0, 0.0).astype(F32)
 
     pending = [
-        functools.partial(step, stage) for stage in range(4) for step in (step_a, step_b)
+        functools.partial(step, stage) for stage in range(1, 4) for step in (step_a, step_b)
     ]
     for at in range(0, joint, BLOCK):
         factor_step(work, at)
-        if pending and at >= BLOCK:
+        if pending:
             pending.pop(0)()
     linv_ref[...] = work[:, joint:]
     for step in pending:
@@ -447,7 +449,7 @@
         ],
         out_specs=(tiled(joint), whole((joint, cols)), tiled(cols)),
         scratch_shapes=[pltpu.VMEM((joint, cols), BF16), pltpu.VMEM((joint, cols), BF16)],
-        compiler_params=pltpu.CompilerParams(vmem_limit_bytes=40 * 1024 * 1024),
+        compiler_params=pltpu.CompilerParams(vmem_limit_bytes=60 * 1024 * 1024),
         name="factors_and_remainder",
     )(descriptors, points, panel_points, sums, inverse)
 

time: 63.3 us -> 59.1 us (0.934)
  local copies, waits for them, and re-layouts: 3.13 us -> 0 us
  Pallas kernels: 59.2 us -> 58.3 us
    unnamed x10 -> x0, local copies, waits for them, and re-layouts: 3.13 us -> none
    pallas_call x1, Pallas kernels: 50.9 us -> 48.2 us  [reduced(): pl.pallas_call(functools.partial(reduce_kernel, n_rows, n_cols, inner, fl...]
    pallas_call x1, Pallas kernels: 8.3 us -> 10.1 us  [finished(): pl.pallas_call(functools.partial(finish_kernel, total_rows), out_shape=(j...]
where the time goes in v3:
time: 59.1 us; the launch traced here: 58.9 us
  Pallas kernels  58.3 us (99%)
  between operations  0.64 us (1%)
    pallas_call x1, Pallas kernels, reduced(): pl.pallas_call(functools.partial(reduce_kernel, n_rows, n_cols, inner, fl...  48.2 us
    pallas_call x1, Pallas kernels, finished(): pl.pallas_call(functools.partial(finish_kernel, total_rows), out_shape=(j...  10.1 us

profile of v3, /device:TPU:0, one launch (start us, length us, event | category | flops | bytes accessed | tf_op | source)
XLA Modules:
  0.0 58.9 jit_solution(5905892460214251313)
XLA Ops:
  0.6 48.2 %gram_and_products.1 = (bf16[256,512]{1,0:T(8,128)(2,1)}, f32[2048,128]{1,0:T(8,128)}, f32[256,256]{1,0:T(8,128)}) custom-call(bf16[1024,512]{1,0:T(8,128)(2,1)} %d_ref.1, bf16[1024,512]{1,0:T(8,128)(2,1)} %p_ref.1), custom_call_target="tpu_custom_call" | custom-call | tf_op jit(solution)/shard_map/gram_and_products/pallas_call | solution.py:361
  48.8 10.1 %factors_and_remainder.1 = (f32[1024,256]{1,0:T(8,128)}, f32[256,1024]{1,0:T(8,128)}, bf16[1024,1024]{1,0:T(8,128)(2,1)}) custom-call(bf16[1024,512]{1,0:T(8,128)(2,1)} %d_ref.1, bf16[1024,512]{1,0:T(8,128)(2,1)} %p_ref.1, bf16[256,512]{1,0:T(8,128)(2,1)} %get-tuple-element.6.pp_ref, f32[2048,128]{1,0:T(8,128)} %get-tuple-element.7.s_ref, ...), custom_call_target="tpu_custom_call" | custom-call | tf_op jit(solution)/shard_map/factors_and_remainder/pallas_call | solution.py:435

commit v4 on v3

--- a/solution.py
+++ b/solution.py
@@ -58,13 +58,14 @@
         ]
         scale = jnp.ones((SUB, LANES), F32)
         for j in range(SUB):
-            pivot = columns[j][j : j + 1, :]
-            factor = jnp.where(rows > j, columns[j] * (1.0 / pivot), 0.0)
+            root = lax.rsqrt(columns[j][j : j + 1, :])
+            reciprocal = root * root
             for k in range(j + 1, SUB):
-                columns[k] = columns[k] - factor * columns[k][j : j + 1, :]
+                columns[k] = columns[k] - (columns[j] * columns[k][j : j + 1, :]) * reciprocal
+            factor = jnp.where(rows > j, columns[j] * reciprocal, 0.0)
             tile = tile - factor * tile[j : j + 1, :]
             inverse = inverse - factor * inverse[j : j + 1, :]
-            scale = jnp.where(rows[:SUB] == j, lax.rsqrt(pivot), scale)
+            scale = jnp.where(rows[:SUB] == j, root, scale)
         done.append(inverse[:SUB] * scale)
         tile, inverse = tile[SUB:], inverse[SUB:]
     return jnp.concatenate(done, axis=0)[:, :BLOCK]
@@ -309,6 +310,11 @@
         gram_own, lambda which: gram.at[which], swap_send, swap_recv, own_gram
     )
     gram_start()
+    results = []
+    if first > 0:
+        head = s_ref.at[pl.ds(0, joint)]
+        results.append(pltpu.make_async_copy(gram_own, head, out_sem.at[2]))
+        results[-1].start()
     step_b(0)
     gram_finish()
     work[:, :PANEL] = gram[0] / total_rows
@@ -322,18 +328,16 @@
     ]
     for at in range(0, joint, BLOCK):
         factor_step(work, at)
-        if pending:
+        if len(pending) > 2:
             pending.pop(0)()
     linv_ref[...] = work[:, joint:]
-    for step in pending:
+    for step in pending[:-2]:
         step()
-    rest = pl.ds(first, part.shape[0] - first)
-    results = [pltpu.make_async_copy(full.at[rest], s_ref.at[rest], out_sem.at[0])]
-    if first > 0:
-        head = s_ref.at[pl.ds(0, joint)]
-        results.append(pltpu.make_async_copy(gram_own, head, out_sem.at[1]))
-    for result in results:
-        result.start()
+    for c, step in enumerate((step_a, step_b)):
+        step(3)
+        rows = pl.ds(first + c * chunk, chunk)
+        results.append(pltpu.make_async_copy(full.at[rows], s_ref.at[rows], out_sem.at[c]))
+        results[-1].start()
     points_drain()
     gram_drain()
     for t in range(1, outer):
@@ -390,7 +394,7 @@
             dma((3, most)),
             dma((2, n_cols - 1)),
             dma((2,)),
-            dma((2,)),
+            dma((3,)),
             dma((2,)),
         ],
         compiler_params=pltpu.CompilerParams(
@@ -407,9 +411,11 @@
 
     @pl.when(pl.program_id(0) == 0)
     def _():
-        for block in range(r_ref.shape[1] // PANEL):
-            cols = slice(block * PANEL, (block + 1) * PANEL)
-            sums = s_ref[block * joint : (block + 1) * joint, :]
+        for block in range(r_ref.shape[1] // joint):
+            cols = slice(block * joint, (block + 1) * joint)
+            at = block * 2 * joint
+            halves = (s_ref[at : at + joint, :], s_ref[at + joint : at + 2 * joint, :])
+            sums = jnp.concatenate(halves, axis=1)
             value = dot_nn(linv_ref[...], sums, HIGHEST) / total_rows
             r_ref[:, cols] = value
             r_high[:, cols], r_low[:, cols] = split(value)

time: 59.1 us -> 56.5 us (0.956)
  Pallas kernels: 58.3 us -> 55.7 us
    pallas_call x1, Pallas kernels: 48.2 us -> 46.3 us  [reduced(): pl.pallas_call(functools.partial(reduce_kernel, n_rows, n_cols, inner, fl...]
    pallas_call x1, Pallas kernels: 10.1 us -> 9.36 us  [finished(): pl.pallas_call(functools.partial(finish_kernel, total_rows), out_shape=(j...]
where the time goes in v4:
time: 56.5 us; the launch traced here: 56.3 us
  Pallas kernels  55.7 us (99%)
  between operations  0.64 us (1%)
    pallas_call x1, Pallas kernels, reduced(): pl.pallas_call(functools.partial(reduce_kernel, n_rows, n_cols, inner, fl...  46.3 us
    pallas_call x1, Pallas kernels, finished(): pl.pallas_call(functools.partial(finish_kernel, total_rows), out_shape=(j...  9.36 us

profile of v4, /device:TPU:0, one launch (start us, length us, event | category | flops | bytes accessed | tf_op | source)
XLA Modules:
  0.0 56.3 jit_solution(16903946577089989424)
XLA Ops:
  0.6 46.3 %gram_and_products.1 = (bf16[256,512]{1,0:T(8,128)(2,1)}, f32[2048,128]{1,0:T(8,128)}, f32[256,256]{1,0:T(8,128)}) custom-call(bf16[1024,512]{1,0:T(8,128)(2,1)} %d_ref.1, bf16[1024,512]{1,0:T(8,128)(2,1)} %p_ref.1), custom_call_target="tpu_custom_call" | custom-call | tf_op jit(solution)/shard_map/gram_and_products/pallas_call | solution.py:365
  47.0 9.4 %factors_and_remainder.1 = (f32[1024,256]{1,0:T(8,128)}, f32[256,1024]{1,0:T(8,128)}, bf16[1024,1024]{1,0:T(8,128)(2,1)}) custom-call(bf16[1024,512]{1,0:T(8,128)(2,1)} %d_ref.1, bf16[1024,512]{1,0:T(8,128)(2,1)} %p_ref.1, bf16[256,512]{1,0:T(8,128)(2,1)} %get-tuple-element.6.pp_ref, f32[2048,128]{1,0:T(8,128)} %get-tuple-element.7.s_ref, ...), custom_call_target="tpu_custom_call" | custom-call | tf_op jit(solution)/shard_map/factors_and_remainder/pallas_call | solution.py:441

commit v5 on v4

--- a/solution.py
+++ b/solution.py
@@ -8,7 +8,7 @@
 from jax.sharding import PartitionSpec as P
 
 PANEL = 128
-BLOCK = 32
+BLOCK = 64
 SUB = 8
 LANES = 128
 HIGHEST = lax.Precision.HIGHEST
@@ -328,7 +328,7 @@
     ]
     for at in range(0, joint, BLOCK):
         factor_step(work, at)
-        if len(pending) > 2:
+        for _ in range(min(2, len(pending) - 2)):
             pending.pop(0)()
     linv_ref[...] = work[:, joint:]
     for step in pending[:-2]:

time: 56.5 us -> 54.9 us (0.972)
  Pallas kernels: 55.7 us -> 54.2 us
    pallas_call x1, Pallas kernels: 46.3 us -> 44.8 us  [reduced(): pl.pallas_call(functools.partial(reduce_kernel, n_rows, n_cols, inner, fl...]
where the time goes in v5:
time: 54.9 us; the launch traced here: 54.8 us
  Pallas kernels  54.2 us (99%)
  between operations  0.64 us (1%)
    pallas_call x1, Pallas kernels, reduced(): pl.pallas_call(functools.partial(reduce_kernel, n_rows, n_cols, inner, fl...  44.8 us
    pallas_call x1, Pallas kernels, finished(): pl.pallas_call(functools.partial(finish_kernel, total_rows), out_shape=(j...  9.35 us

profile of v5, /device:TPU:0, one launch (start us, length us, event | category | flops | bytes accessed | tf_op | source)
XLA Modules:
  0.0 54.8 jit_solution(1086583297815638927)
XLA Ops:
  0.6 44.8 %gram_and_products.1 = (bf16[256,512]{1,0:T(8,128)(2,1)}, f32[2048,128]{1,0:T(8,128)}, f32[256,256]{1,0:T(8,128)}) custom-call(bf16[1024,512]{1,0:T(8,128)(2,1)} %d_ref.1, bf16[1024,512]{1,0:T(8,128)(2,1)} %p_ref.1), custom_call_target="tpu_custom_call" | custom-call | tf_op jit(solution)/shard_map/gram_and_products/pallas_call | solution.py:365
  45.4 9.4 %factors_and_remainder.1 = (f32[1024,256]{1,0:T(8,128)}, f32[256,1024]{1,0:T(8,128)}, bf16[1024,1024]{1,0:T(8,128)(2,1)}) custom-call(bf16[1024,512]{1,0:T(8,128)(2,1)} %d_ref.1, bf16[1024,512]{1,0:T(8,128)(2,1)} %p_ref.1, bf16[256,512]{1,0:T(8,128)(2,1)} %get-tuple-element.6.pp_ref, f32[2048,128]{1,0:T(8,128)} %get-tuple-element.7.s_ref, ...), custom_call_target="tpu_custom_call" | custom-call | tf_op jit(solution)/shard_map/factors_and_remainder/pallas_call | solution.py:441
